TPU v7x, 256 devices: a whole 4x4x8 slice. The times are simulated.
256 devices in a mesh: span: 16 (over y, z_lo), seq: 16 (over z_hi, x, core).
Axes of the slice: x: 4, y: 4, z: 8 (z_hi: 2, z_lo: 4; z = z_hi * 4 + z_lo), core: 2. Of those that a mesh axis runs over, the one named last changes fastest.
Arguments:
- qkv: bfloat16 [16, 2048, 3, 4096], P('span', 'seq'), may hold values from -10 to 10
- timestep: int32 [16], P('span'), may hold values from 0 to 49
- offsets: int32 [16], P('span'), may hold values from 0 to 13, as said below
- gate_table: float32 [50, 4096], replicated, may hold values from 0.5 to 4
Outputs:
- attended: bfloat16 [16, 2048, 4096], P('span', 'seq')
Inputs may be any that keep to these rules, and one draw needn't show every extreme that they name: max(0, c - 2) <= offsets[c] <= min(c, 13); the last span has offsets equal to 13.
All inputs are finite; a program needn't handle non-finite values.
Results may differ from a plain program's by a relative error of at most 0.0031.
Values may be sent and summed in bfloat16 or wider, within the bound.
A program may use at most 128 MiB of HBM per device.

v0:
```python
import math

import jax
import jax.numpy as jnp
from jax import lax
from jax.sharding import PartitionSpec as P

HD = 128
WIN = 2


def passed_along(value, axis, steps):
    count = lax.axis_size(axis)
    first, last = (max(0, -steps), min(count, count - steps))
    return lax.ppermute(value, axis, [(source, source + steps) for source in range(first, last)])


def earlier_blocks(pair_rows):
    received = []
    for distance in range(WIN):
        received.append(passed_along(pair_rows, "span", distance + 1))
    return received


def attend(queries, own_pair, earlier, span_index, first_allowed, gate_row):
    token_count = queries.shape[0]
    head_cols = queries.shape[1]
    local_heads = head_cols // HD
    block_rows = min(512, token_count)
    scale_factor = 1.0 / math.sqrt(HD)
    query_blocks = queries.reshape(token_count // block_rows, block_rows, local_heads, HD)
    gate_shaped = gate_row.reshape(local_heads, 1, HD)

    def scores_of(query_block, pair):
        key_rows = pair[:, 0, :].reshape(token_count, local_heads, HD)
        return (
            jnp.einsum("qhd,khd->hqk", query_block, key_rows, preferred_element_type=jnp.float32)
            * scale_factor
        )

    def weighted(probabilities, pair):
        value_rows = pair[:, 1, :].reshape(token_count, local_heads, HD)
        return jnp.einsum(
            "hqk,khd->hqd",
            probabilities.astype(jnp.bfloat16),
            value_rows,
            preferred_element_type=jnp.float32,
        )

    def one_block(query_block):
        scores = scores_of(query_block, own_pair)
        running = jnp.max(scores, axis=2, keepdims=True)
        probabilities = jnp.exp(scores - running)
        state = (
            running,
            jnp.sum(probabilities, axis=2, keepdims=True),
            weighted(probabilities, own_pair),
        )
        for distance in range(1, WIN + 1):
            allowed = span_index - distance >= first_allowed

            def update(carried, pair=earlier[distance - 1]):
                running, denominator, numerator = carried
                scores = scores_of(query_block, pair)
                newmax = jnp.maximum(running, jnp.max(scores, axis=2, keepdims=True))
                factor = jnp.exp(running - newmax)
                probabilities = jnp.exp(scores - newmax)
                return (
                    newmax,
                    denominator * factor + jnp.sum(probabilities, axis=2, keepdims=True),
                    numerator * factor + weighted(probabilities, pair),
                )

            state = lax.cond(allowed, update, lambda carried: carried, state)
        running, denominator, numerator = state
        return (numerator / denominator * gate_shaped).astype(jnp.bfloat16)

    outputs = lax.map(one_block, query_blocks)
    return jnp.transpose(outputs, (0, 2, 1, 3)).reshape(token_count, head_cols)


def body(qkv, timestep, offsets, gate_table):
    span_index = lax.axis_index("span")
    seq_index = lax.axis_index("seq")
    exchanged = lax.all_to_all(qkv, "seq", split_axis=3, concat_axis=1, tiled=True)[0]
    queries = exchanged[:, 0, :]
    own_pair = exchanged[:, 1:3, :]
    earlier = earlier_blocks(own_pair)
    head_cols = queries.shape[1]
    gate_full = lax.dynamic_slice_in_dim(gate_table, timestep[0], 1, 0)[0]
    gate_row = lax.dynamic_slice_in_dim(gate_full, seq_index * head_cols, head_cols, 0)
    outcome = attend(queries, own_pair, earlier, span_index, offsets[0], gate_row)
    return lax.all_to_all(outcome[None], "seq", split_axis=1, concat_axis=2, tiled=True)


def solution(mesh):
    return jax.shard_map(
        body,
        mesh=mesh,
        in_specs=(P("span", "seq", None, None), P("span"), P("span"), P()),
        out_specs=P("span", "seq", None),
        check_vma=False,
    )
```

profile of v0, /device:TPU:120, one launch (start us, length us, event | category | flops | bytes accessed | tf_op | source)
XLA Modules:
  0.0 386.7 jit_solution(16231366701263214425)
XLA Ops:
  0.0 7.2 %copy.34 = bf16[1,128,3,4096]{1,2,0,3:T(4,128)(2,1)} copy(bf16[1,128,3,4096]{3,1,2,0:T(8,128)(2,1)} %param.10) | data formatting | bytes 6291456 | tf_op args[0]
  7.2 106.8 %all_to_all.33 = bf16[1,128,3,4096]{1,2,0,3:T(4,128)(2,1)S(1)} all-to-all(bf16[1,128,3,4096]{1,2,0,3:T(4,128)(2,1)} %copy.34), channel_id=1, replica_groups=mesh['span'=16,'seq'=16] {'seq'}, dimensions={3} | all-to-all | bytes 6291456 | tf_op jit(solution)/shard_map/all_to_all | solution.py:85
  114.0 4.3 %copy.35 = bf16[1,16,128,3,256]{2,1,4,3,0:T(8,128)(2,1)} copy(bf16[1,16,128,3,256]{2,3,4,1,0:T(4,128)(2,1)S(1)} %bitcast.99) | data formatting | bytes 6291456 | tf_op jit(solution)/shard_map/all_to_all | solution.py:85
  118.3 5.8 %squeeze.39 = bf16[2048,3,256]{0,2,1:T(8,128)(2,1)} reshape(bf16[1,16,128,3,256]{2,1,4,3,0:T(8,128)(2,1)} %copy.35) | data formatting | bytes 6291456 | tf_op jit(solution)/shard_map/squeeze | solution.py:85
  124.1 1.8 slice.31
  133.7 2.7 copy.37
  136.4 38.4 %collective-permute-done = bf16[2048,2,256]{0,2,1:T(8,128)(2,1)} collective-permute-done((bf16[2048,2,256]{0,2,1:T(8,128)(2,1)S(1)}, bf16[2048,2,256]{0,2,1:T(8,128)(2,1)}, u32[]{:S(2)}, u32[]{:S(2)}) %collective-permute-start) | collective-permute-done | bytes 2097184 | tf_op jit(solution)/shard_map/ppermute | solution.py:15
  174.7 90.7 %collective-permute-done.1 = bf16[2048,2,256]{0,2,1:T(8,128)(2,1)} collective-permute-done((bf16[2048,2,256]{0,2,1:T(8,128)(2,1)S(1)}, bf16[2048,2,256]{0,2,1:T(8,128)(2,1)}, u32[]{:S(2)}, u32[]{:S(2)}) %collective-permute-start.1) | collective-permute-done | bytes 2097184 | tf_op jit(solution)/shard_map/ppermute | solution.py:15
  265.5 79.9 %while.12 = (s32[]{:T(128)}, bf16[4,2,512,128]{3,2,1,0:T(8,128)(2,1)}, pred[]{:T(512)}, pred[]{:T(512)}, bf16[4,512,2,128]{3,1,2,0:T(8,128)(2,1)}, /*index=5*/bf...) while((s32[]{:T(128)}, ...), condition=%wide.region_11.12_spmd, body=%wide.region_0.11_spmd.sunk | while | flops 3272478720 | bytes 99235616 | solution.py:78
  271.2 6.7 %conditional.4 = ((f32[2,512,1]{1,0,2:T(2,128)S(1)}, f32[2,512,1]{1,0,2:T(2,128)S(1)}, f32[2,512,128]{2,1,0:T(8,128)S(1)})) conditional(s32[]{:T(128)} %convert_element_type.46, (f32[2,512,1]{1,0,2:T(2,128)S(1)}, f32[2,512,1]{1,0,2:T(2,128)S(1)}, f32[2,512,128]{2,1,0:T(8,128)S(1)}) %tuple.75, (bf16[2048,2,256]{0,2,1:T(8,128)(2,1)}, ...), branch_computations={%region_3.3_spmd, %region_4.6_spmd} | conditional | flops 1090784256 | bytes 32833568 | solution.py:74
  275.9 1.9 fusion.6
  277.9 6.7 %conditional.5 = ((f32[2,512,1]{1,0,2:T(2,128)S(1)}, f32[2,512,128]{2,1,0:T(8,128)S(1)})) conditional(s32[]{:T(128)} %convert_element_type.45, (f32[2,512,1]{1,0,2:T(2,128)S(1)}, f32[2,512,128]{2,1,0:T(8,128)S(1)}) %tuple.60, (bf16[2048,2,256]{0,2,1:T(8,128)(2,1)}, bf16[512,2,128]{2,0,1:T(8,128)(2,1)S(1)}, f32[2,512,1]{1,0,2:T(2,128)S(1)}, ...), branch_computations={%region_7.7_spmd, %region_8.10_spmd} | conditional | flops 1090784256 | bytes 32825368 | solution.py:74
  277.9 1.7 fusion.30
  282.6 1.9 fusion.17
  291.2 6.7 %conditional.4 = ((f32[2,512,1]{1,0,2:T(2,128)S(1)}, f32[2,512,1]{1,0,2:T(2,128)S(1)}, f32[2,512,128]{2,1,0:T(8,128)S(1)})) conditional(s32[]{:T(128)} %convert_element_type.46, (f32[2,512,1]{1,0,2:T(2,128)S(1)}, f32[2,512,1]{1,0,2:T(2,128)S(1)}, f32[2,512,128]{2,1,0:T(8,128)S(1)}) %tuple.75, (bf16[2048,2,256]{0,2,1:T(8,128)(2,1)}, ...), branch_computations={%region_3.3_spmd, %region_4.6_spmd} | conditional | flops 1090784256 | bytes 32833568 | solution.py:74
  291.2 1.7 fusion.31
  295.9 1.9 fusion.6
  297.9 6.7 %conditional.5 = ((f32[2,512,1]{1,0,2:T(2,128)S(1)}, f32[2,512,128]{2,1,0:T(8,128)S(1)})) conditional(s32[]{:T(128)} %convert_element_type.45, (f32[2,512,1]{1,0,2:T(2,128)S(1)}, f32[2,512,128]{2,1,0:T(8,128)S(1)}) %tuple.60, (bf16[2048,2,256]{0,2,1:T(8,128)(2,1)}, bf16[512,2,128]{2,0,1:T(8,128)(2,1)S(1)}, f32[2,512,1]{1,0,2:T(2,128)S(1)}, ...), branch_computations={%region_7.7_spmd, %region_8.10_spmd} | conditional | flops 1090784256 | bytes 32825368 | solution.py:74
  302.6 1.9 fusion.17
  311.1 6.7 %conditional.4 = ((f32[2,512,1]{1,0,2:T(2,128)S(1)}, f32[2,512,1]{1,0,2:T(2,128)S(1)}, f32[2,512,128]{2,1,0:T(8,128)S(1)})) conditional(s32[]{:T(128)} %convert_element_type.46, (f32[2,512,1]{1,0,2:T(2,128)S(1)}, f32[2,512,1]{1,0,2:T(2,128)S(1)}, f32[2,512,128]{2,1,0:T(8,128)S(1)}) %tuple.75, (bf16[2048,2,256]{0,2,1:T(8,128)(2,1)}, ...), branch_computations={%region_3.3_spmd, %region_4.6_spmd} | conditional | flops 1090784256 | bytes 32833568 | solution.py:74
  315.9 1.9 fusion.6
  317.8 6.7 %conditional.5 = ((f32[2,512,1]{1,0,2:T(2,128)S(1)}, f32[2,512,128]{2,1,0:T(8,128)S(1)})) conditional(s32[]{:T(128)} %convert_element_type.45, (f32[2,512,1]{1,0,2:T(2,128)S(1)}, f32[2,512,128]{2,1,0:T(8,128)S(1)}) %tuple.60, (bf16[2048,2,256]{0,2,1:T(8,128)(2,1)}, bf16[512,2,128]{2,0,1:T(8,128)(2,1)S(1)}, f32[2,512,1]{1,0,2:T(2,128)S(1)}, ...), branch_computations={%region_7.7_spmd, %region_8.10_spmd} | conditional | flops 1090784256 | bytes 32825368 | solution.py:74
  317.9 1.7 fusion.30
  322.6 1.9 fusion.17
  331.1 6.7 %conditional.4 = ((f32[2,512,1]{1,0,2:T(2,128)S(1)}, f32[2,512,1]{1,0,2:T(2,128)S(1)}, f32[2,512,128]{2,1,0:T(8,128)S(1)})) conditional(s32[]{:T(128)} %convert_element_type.46, (f32[2,512,1]{1,0,2:T(2,128)S(1)}, f32[2,512,1]{1,0,2:T(2,128)S(1)}, f32[2,512,128]{2,1,0:T(8,128)S(1)}) %tuple.75, (bf16[2048,2,256]{0,2,1:T(8,128)(2,1)}, ...), branch_computations={%region_3.3_spmd, %region_4.6_spmd} | conditional | flops 1090784256 | bytes 32833568 | solution.py:74
  331.1 1.7 fusion.31
  335.9 1.9 fusion.6
  337.8 6.7 %conditional.5 = ((f32[2,512,1]{1,0,2:T(2,128)S(1)}, f32[2,512,128]{2,1,0:T(8,128)S(1)})) conditional(s32[]{:T(128)} %convert_element_type.45, (f32[2,512,1]{1,0,2:T(2,128)S(1)}, f32[2,512,128]{2,1,0:T(8,128)S(1)}) %tuple.60, (bf16[2048,2,256]{0,2,1:T(8,128)(2,1)}, bf16[512,2,128]{2,0,1:T(8,128)(2,1)S(1)}, f32[2,512,1]{1,0,2:T(2,128)S(1)}, ...), branch_computations={%region_7.7_spmd, %region_8.10_spmd} | conditional | flops 1090784256 | bytes 32825368 | solution.py:74
  342.6 1.9 fusion.17
  345.4 2.3 copy.38
  348.7 10.6 %reduce = bf16[2048,256]{1,0:T(8,128)(2,1)S(1)} reduce(bf16[2048,1,256]{2,1,0:T(2,128)(2,1)S(1)} %bitcast.101, bf16[]{:T(256)} %broadcast.34), dimensions={1}, to_apply=%bitcast.54.reduce_sub_computation | reduce | bytes 2097154
  359.6 23.9 %all_to_all.34 = bf16[16,2,16384]{2,1,0:T(2,128)(2,1)S(1)} all-to-all(bf16[16,2,16384]{2,1,0:T(2,128)(2,1)S(1)} %reshape.9), channel_id=1, replica_groups=mesh['span'=16,'seq'=16] {'seq'}, dimensions={0} | all-to-all | bytes 2097152 | tf_op jit(solution)/shard_map/all_to_all | solution.py:93
  (77 shorter events, 68.3 us)
Async XLA Ops:
  125.9 48.8 %collective-permute-start = (bf16[2048,2,256]{0,2,1:T(8,128)(2,1)S(1)}, bf16[2048,2,256]{0,2,1:T(8,128)(2,1)}, u32[]{:S(2)}, u32[]{:S(2)}) collective-permute-start(bf16[2048,2,256]{0,2,1:T(8,128)(2,1)S(1)} %slice.31), channel_id=1, source_target_pairs={{0,16},{16,32},{32,48},{48,64},{64,80},{80,96},{96,112},{112,128},... | collective-permute-start | bytes 6291464 | tf_op jit(solution)/shard_map/ppermute | solution.py:15
  127.2 138.3 %collective-permute-start.1 = (bf16[2048,2,256]{0,2,1:T(8,128)(2,1)S(1)}, bf16[2048,2,256]{0,2,1:T(8,128)(2,1)}, u32[]{:S(2)}, u32[]{:S(2)}) collective-permute-start(bf16[2048,2,256]{0,2,1:T(8,128)(2,1)S(1)} %slice.31), channel_id=1, source_target_pairs={{0,32},{16,48},{32,64},{48,80},{64,96},{80,112},{96,128},{112,144}... | collective-permute-start | bytes 6291464 | tf_op jit(solution)/shard_map/ppermute | solution.py:15
where the time goes:
time: 388 us; the launch traced here: 387 us
  blocking collectives  131 us (34%)
  waiting for transfers between devices  129 us (33%)
  local copies, waits for them, and re-layouts  50.4 us (13%)
  matrix products  37.6 us (10%)
  other arithmetic  34.2 us (9%)
    ppermute x2, waiting for transfers between devices, passed_along(): lax.ppermute(value, axis, [(source, source + steps) for source in range(f...  129 us
    all_to_all x1, blocking collectives, body(): lax.all_to_all(qkv, 'seq', split_axis=3, concat_axis=1, tiled=True)[0]  107 us
    all_to_all x1, blocking collectives, body(): lax.all_to_all(outcome[None], 'seq', split_axis=1, concat_axis=2, tiled=T...  23.9 us
    dot_general x12, matrix products, weighted(): jnp.einsum('hqk,khd->hqd', probabilities.astype(jnp.bfloat16), value_rows...  21.6 us
    dot_general x12, matrix products, scores_of(): jnp.einsum('qhd,khd->hqk', query_block, key_rows, preferred_element_type=...  16 us
    slice x12, local copies, waits for them, and re-layouts, weighted(): value_rows = pair[:, 1, :].reshape(token_count, local_heads, HD)  14.3 us
    reduce_sum x8, other arithmetic, update(): jnp.sum(probabilities, axis=2, keepdims=True)  13.2 us
    unnamed x1, other arithmetic  10.6 us
  transfers between devices with their start and end apart: 2, of which 2 were waited for; matrix products, arithmetic and copies ran while one was open for 2% of the time, Pallas kernels for 0%

commit v1 on v0

v1 whole, which is shorter than its diff:
```python
import functools
import math

import jax
import jax.numpy as jnp
from jax import lax
from jax.experimental import pallas as pl
from jax.experimental.pallas import tpu as pltpu
from jax.sharding import PartitionSpec as P

HD = 128
WIN = 2
SLOTS = WIN + 1
PAIR = 2
TOK = 128
LANES = 8
HALF = LANES * TOK
ROWS = 2 * HALF
SCALE = math.log2(math.e) / math.sqrt(HD)
MESH = pl.DeviceIdType.MESH


def device(y, z, xc):
    return (y * 4 + z % 4, (z // 4) * 8 + xc)


def kernel(
    qkv, timestep, offsets, gate_table, out,
    queries, pairs, results, gates, row_max, row_sum, total,
    pair_recv, query_recv, out_recv, gate_sem,
    near_send, far_send, query_near_send, query_far_send, chain_send, out_near_send, out_far_send,
):
    span = lax.axis_index("span")
    seq = lax.axis_index("seq")
    y, z_lo = span // 4, span % 4
    z_hi, xc = seq // 8, seq % 8
    z = z_hi * 4 + z_lo
    group = (z_hi + y) % 2

    across = (z + 4) % 8
    drop_y, drop_z = (y + z_lo // 2) % 4, (z + 6) % 8
    source_y, source_z = (y + 3 + z_lo // 2) % 4, (z + 2) % 8
    following = device((y + (z_lo + 1) // 4) % 4, (z + 1) % 8, xc)
    previous = device((y + 3 + (z_lo + 3) // 4) % 4, (z + 7) % 8, xc)

    barrier = pltpu.get_barrier_semaphore()
    greeted = [following, previous]
    for turn in range(LANES):
        lane = (xc + turn) % LANES
        if turn:
            greeted.append(device(y, z, lane))
        greeted.append(device(y, across, lane))
        greeted.append(device(drop_y, drop_z, lane))
        greeted.append(device(source_y, source_z, lane))
    for other in greeted:
        pl.semaphore_signal(barrier, inc=1, device_id=other, device_id_type=MESH)
    pl.semaphore_wait(barrier, len(greeted))

    own_rows = pl.ds(pl.multiple_of(xc * TOK, TOK), TOK)
    far_rows = pl.ds(pl.multiple_of(HALF + xc * TOK, TOK), TOK)

    def columns(lane, which, head):
        return pl.ds(pl.multiple_of((lane * 2 + which) * (PAIR * HD) + head * HD, HD), HD)

    def send(src, dst, send_sem, recv_sem, target):
        pltpu.make_async_remote_copy(
            src_ref=src, dst_ref=dst, send_sem=send_sem, recv_sem=recv_sem,
            device_id=target, device_id_type=MESH,
        ).start()

    def wait_bytes(ref, sem):
        pltpu.make_async_copy(ref, ref, sem).wait()

    def scatter(head):
        for turn in range(LANES):
            lane = (xc + turn) % LANES
            send(
                qkv.at[1:3, :, columns(lane, 1 - group, head)],
                pairs.at[head, 2, 1, :, own_rows, :],
                far_send.at[head], pair_recv.at[head, 2, 1], device(drop_y, drop_z, lane),
            )
        for turn in range(LANES):
            lane = (xc + turn) % LANES
            src = qkv.at[1:3, :, columns(lane, group, head)]
            dst = pairs.at[head, 0, 0, :, own_rows, :]
            if turn:
                send(src, dst, near_send.at[head], pair_recv.at[head, 0, 0], device(y, z, lane))
            else:
                pltpu.make_async_copy(src, dst, pair_recv.at[head, 0, 0]).start()
        for turn in range(LANES):
            lane = (xc + turn) % LANES
            send(
                qkv.at[0, :, columns(lane, 1 - group, head)],
                queries.at[head, far_rows, :],
                query_far_send.at[head], query_recv.at[head], device(y, across, lane),
            )
        for turn in range(LANES):
            lane = (xc + turn) % LANES
            src = qkv.at[0, :, columns(lane, group, head)]
            dst = queries.at[head, own_rows, :]
            if turn:
                send(src, dst, query_near_send.at[head], query_recv.at[head], device(y, z, lane))
            else:
                pltpu.make_async_copy(src, dst, query_recv.at[head]).start()

    def arrived(head, slot, half):
        wait_bytes(pairs.at[head, slot, half], pair_recv.at[head, slot, half])

    def pass_on(head, slot, half):
        arrived(head, slot, half)
        to = slot + 1 if half == 0 else slot - 1
        send(
            pairs.at[head, slot, half], pairs.at[head, to, half],
            chain_send.at[head, slot, half], pair_recv.at[head, to, half],
            following if half == 0 else previous,
        )

    def attend(head, slot, half, part):
        rows = pl.ds(part * HALF, HALF)
        scores = lax.dot_general(
            queries[head, rows, :], pairs[head, slot, half, 0],
            (((1,), (1,)), ((), ())), preferred_element_type=jnp.float32,
        )
        old = row_max[head, rows, :]
        new = jnp.maximum(old, jnp.broadcast_to(jnp.max(scores, axis=1, keepdims=True), old.shape))
        scale, shift = jnp.float32(SCALE), new * SCALE
        if slot:
            allowed = span - slot >= offsets[0]
            new = jnp.where(allowed, new, old)
            scale = jnp.where(allowed, scale, 0.0)
            shift = jnp.where(allowed, shift, 1e30)
        factor = jnp.exp2((old - new) * SCALE)
        weights = jnp.exp2(scores * scale - shift[:, :1])
        partial = weights[:, :HD]
        for block in range(1, HALF // HD):
            partial = partial + weights[:, block * HD : (block + 1) * HD]
        row_sum[head, rows, :] = row_sum[head, rows, :] * factor + partial
        total[head, rows, :] = total[head, rows, :] * factor + jnp.dot(
            weights.astype(jnp.bfloat16), pairs[head, slot, half, 1], preferred_element_type=jnp.float32
        )
        row_max[head, rows, :] = new

    def attend_all(head, slot, half):
        def step(part, carry):
            attend(head, slot, half, part)
            return carry

        lax.fori_loop(0, 2, step, 0)

    def finish(head, part):
        rows = pl.ds(part * HALF, HALF)
        row = lax.broadcasted_iota(jnp.int32, gates.shape, 0) == timestep[0]
        gate = jnp.sum(jnp.where(row, gates[...], 0.0), axis=0, keepdims=True)[:, head * HD : (head + 1) * HD]
        denominator = jnp.sum(row_sum[head, rows, :], axis=1, keepdims=True)
        results[head, rows, :] = (total[head, rows, :] / denominator * gate).astype(jnp.bfloat16)
        for turn in range(LANES):
            lane = (xc + turn) % LANES
            src = results.at[head, pl.ds(pl.multiple_of(part * HALF + lane * TOK, TOK), TOK), :]
            dst = out.at[:, columns(xc, group, head)]
            if part:
                send(src, dst, out_far_send.at[head], out_recv, device(y, across, lane))
            elif turn:
                send(src, dst, out_near_send.at[head], out_recv, device(y, z, lane))
            else:
                pltpu.make_async_copy(src, dst, out_recv).start()

    def finish_with(head, slot, half):
        for part in (1, 0):
            attend(head, slot, half, part)
            finish(head, part)

    gate_copy = pltpu.make_async_copy(
        gate_table.at[:, pl.ds(pl.multiple_of((xc * 2 + group) * (PAIR * HD), PAIR * HD), PAIR * HD)], gates, gate_sem
    )
    scatter(0)
    scatter(1)
    gate_copy.start()
    row_max[...] = jnp.full_like(row_max, -1e30)
    row_sum[...] = jnp.zeros_like(row_sum)
    total[...] = jnp.zeros_like(total)
    gate_copy.wait()

    pass_on(0, 0, 0)
    pass_on(0, 2, 1)
    pass_on(1, 0, 0)
    wait_bytes(queries.at[0], query_recv.at[0])
    attend_all(0, 0, 0)
    pass_on(0, 1, 0)
    pass_on(0, 1, 1)
    attend_all(0, 2, 1)
    pass_on(1, 2, 1)
    attend_all(0, 1, 0)
    pass_on(1, 1, 0)
    attend_all(0, 1, 1)
    pass_on(1, 1, 1)
    arrived(0, 2, 0)
    attend_all(0, 2, 0)
    wait_bytes(queries.at[1], query_recv.at[1])
    attend_all(1, 0, 0)
    arrived(0, 0, 1)
    finish_with(0, 0, 1)
    attend_all(1, 2, 1)
    attend_all(1, 1, 0)
    attend_all(1, 1, 1)
    arrived(1, 2, 0)
    attend_all(1, 2, 0)
    arrived(1, 0, 1)
    finish_with(1, 0, 1)

    for head in range(PAIR):
        wait_bytes(pairs.at[head, 0, 0], far_send.at[head])
        wait_bytes(pairs.at[head, 0, 0, :, : HALF - TOK, :], near_send.at[head])
        wait_bytes(queries.at[head, :HALF, :], query_far_send.at[head])
        wait_bytes(queries.at[head, : HALF - TOK, :], query_near_send.at[head])
        for slot, half in ((0, 0), (1, 0), (1, 1), (2, 1)):
            wait_bytes(pairs.at[head, slot, half], chain_send.at[head, slot, half])
        wait_bytes(results.at[head, :HALF, :], out_far_send.at[head])
        wait_bytes(results.at[head, : HALF - TOK, :], out_near_send.at[head])
    wait_bytes(out, out_recv)


def body(qkv, timestep, offsets, gate_table):
    stacked = jnp.transpose(qkv[0], (1, 0, 2))
    anywhere = pl.BlockSpec(memory_space=pl.ANY)
    scalar = pl.BlockSpec(memory_space=pltpu.SMEM)
    dma = pltpu.SemaphoreType.DMA
    out = pl.pallas_call(
        kernel,
        out_shape=jax.ShapeDtypeStruct((TOK, qkv.shape[3]), jnp.bfloat16),
        in_specs=[anywhere, scalar, scalar, anywhere],
        out_specs=anywhere,
        scratch_shapes=[
            pltpu.VMEM((PAIR, ROWS, HD), jnp.bfloat16),
            pltpu.VMEM((PAIR, SLOTS, 2, 2, HALF, HD), jnp.bfloat16),
            pltpu.VMEM((PAIR, ROWS, HD), jnp.bfloat16),
            pltpu.VMEM((gate_table.shape[0], PAIR * HD), jnp.float32),
            pltpu.VMEM((PAIR, ROWS, HD), jnp.float32),
            pltpu.VMEM((PAIR, ROWS, HD), jnp.float32),
            pltpu.VMEM((PAIR, ROWS, HD), jnp.float32),
            dma((PAIR, SLOTS, 2)),
            dma((PAIR,)),
            dma,
            dma,
            dma((PAIR,)),
            dma((PAIR,)),
            dma((PAIR,)),
            dma((PAIR,)),
            dma((PAIR, SLOTS, 2)),
            dma((PAIR,)),
            dma((PAIR,)),
        ],
        compiler_params=pltpu.CompilerParams(
            collective_id=0, has_side_effects=True, vmem_limit_bytes=56 * 1024 * 1024
        ),
        cost_estimate=pl.CostEstimate(
            flops=4 * PAIR * ROWS * SLOTS * ROWS * HD,
            bytes_accessed=4 * 1024 * 1024,
            transcendentals=PAIR * ROWS * SLOTS * ROWS,
        ),
        name="span_attention",
    )(stacked, timestep, offsets, gate_table)
    return out[None]


def solution(mesh):
    return jax.shard_map(
        body,
        mesh=mesh,
        in_specs=(P("span", "seq", None, None), P("span"), P("span"), P()),
        out_specs=P("span", "seq", None),
        check_vma=False,
    )
```

time: 388 us -> 166 us (0.43)
  the two profiles are of different devices: /device:TPU:120 before, /device:TPU:1 now
where the time goes in v1:
time: 166 us; the launch traced here: 163 us
  Pallas kernels  159 us (96%)
  local copies, waits for them, and re-layouts  2.29 us (1%)
    pallas_call x1, Pallas kernels, body(): pl.pallas_call(kernel, out_shape=jax.ShapeDtypeStruct((TOK, qkv.shape[3])...  159 us

profile of v1, /device:TPU:1, one launch (start us, length us, event | category | flops | bytes accessed | tf_op | source)
XLA Modules:
  0.0 162.7 jit_solution(15980990607367305462)
XLA Ops:
  1.3 159.1 %span_attention.1 = bf16[128,4096]{1,0:T(8,128)(2,1)} custom-call(bf16[3,128,4096]{2,1,0:T(8,128)(2,1)} %bitcast.5, s32[1]{0:T(128)S(6)} %copy.6.timestep, s32[1]{0:T(128)S(6)} %copy.7.offsets, f32[50,4096]{1,0:T(8,128)} %gate_table.1), custom_call_target="tpu_custom_call" | custom-call | flops 12884901888 | bytes 4194304 | tf_op jit(solution)/shard_map/span_attention/pallas_call | solution.py:227
  160.4 2.3 %copy.8 = bf16[1,128,4096]{2,1,0:T(8,128)(2,1)} copy(bf16[1,128,4096]{2,1,0:T(8,128)(2,1)} %bitcast.4) | data formatting | bytes 2097152

commit v2 on v0

v2 whole, which is shorter than its diff:
```python
import math

import jax
import jax.numpy as jnp
from jax import lax
from jax.experimental import pallas as pl
from jax.experimental.pallas import tpu as pltpu
from jax.sharding import PartitionSpec as P

HD = 128
WIN = 2
OWN = 2
SLOTS = OWN + WIN
SOURCES = 16
TOK = 128
ROWS = SOURCES * TOK
CHIPS = 32
PARTS = 2
PART = TOK // PARTS
KEYS = SOURCES * PART
TILE = 256
SCALE = math.log2(math.e) / math.sqrt(HD)
MESH = pl.DeviceIdType.MESH


def device(y, z, x, core):
    return (y * 4 + z % 4, (z // 4) * 8 + x * 2 + core)


def kernel(
    qkv, timestep, offsets, gate_table, out,
    queries, pairs, results, gates, note, notes, row_max, total,
    query_recv, pair_recv, out_recv, note_recv, gate_sem,
    query_send, pair_send, out_send, note_send, chain_send,
    query_near_send, pair_near_send, out_near_send,
):
    span = lax.axis_index("span")
    seq = lax.axis_index("seq")
    y, z_lo = span // 4, span % 4
    z_hi, x, core = seq // 8, seq // 2 % 4, seq % 2
    z = z_hi * 4 + z_lo
    head = x * 8 + z
    home = z_lo // 2
    first_span = y * 4 + core * OWN
    at_home = core == home
    following = device((y + core) % 4, z, x, 1 - core)
    beyond = device((y + 3 + 2 * core) % 4, z, x, 1 - core)

    barrier = pltpu.get_barrier_semaphore()
    greeted = [beyond]
    for turn in range(CHIPS):
        for other in range(2):
            if turn or other:
                greeted.append(device(y, (z + turn) % 8, (x + turn // 8) % 4, (core + other) % 2))
    for other in greeted:
        pl.semaphore_signal(barrier, inc=1, device_id=other, device_id_type=MESH)
    pl.semaphore_wait(barrier, len(greeted))

    def columns(which):
        return pl.ds(pl.multiple_of(which * HD, HD), HD)

    def remote(src, dst, send_sem, recv_sem, target):
        return pltpu.make_async_remote_copy(
            src_ref=src, dst_ref=dst, send_sem=send_sem, recv_sem=recv_sem,
            device_id=target, device_id_type=MESH,
        )

    def here_or_there(stays, src, dst, send_sem, recv_sem, target):
        @pl.when(stays)
        def _():
            pltpu.make_async_copy(src, dst, recv_sem).start()

        @pl.when(jnp.logical_not(stays))
        def _():
            remote(src, dst, send_sem, recv_sem, target).start()

    def wait_bytes(ref, sem):
        pltpu.make_async_copy(ref, ref, sem).wait()

    def scatter(source, dst, send_sem, near_sem, recv_sem):
        here_or_there(at_home, source(head), dst, near_sem, recv_sem, device(y, z, x, home))

        def step(turn, carry):
            to_z, to_x = (z + turn) % 8, (x + turn // 8) % 4
            remote(source(to_x * 8 + to_z), dst, send_sem, recv_sem, device(y, to_z, to_x, home)).start()
            return carry

        lax.fori_loop(1, CHIPS, step, 0)

    mine = z_lo % 2
    def scatter_queries():
        scatter(
            lambda which: qkv.at[0, :, columns(which)],
            queries.at[mine, pl.ds(pl.multiple_of(seq * TOK, TOK), TOK), :],
            query_send, query_near_send, query_recv.at[mine],
        )

    def scatter_pairs(part):
        scatter(
            lambda which: qkv.at[1:3, pl.ds(part * PART, PART), columns(which)],
            pairs.at[WIN + mine, part, :, pl.ds(pl.multiple_of(seq * PART, PART), PART), :],
            pair_send.at[part], pair_near_send.at[part], pair_recv.at[WIN + mine, part],
        )

    def pass_on(own, part):
        wait_bytes(pairs.at[WIN + own, part], pair_recv.at[WIN + own, part])
        remote(
            pairs.at[WIN + own, part], pairs.at[own, part],
            chain_send.at[own, part], pair_recv.at[own, part], following,
        ).start()

    def attend(own, slot, part):
        allowed = first_span + slot - WIN >= notes[own, 1, 0:1, 0:1]
        scale = jnp.where(allowed, jnp.float32(SCALE), 0.0)
        keys = pairs[slot, part, 0]
        values = jnp.concatenate([pairs[slot, part, 1], jnp.ones((KEYS, HD), jnp.bfloat16)], axis=1)

        def rows(tile):
            return pl.ds(tile * TILE, TILE)

        def scores_of(tile):
            return lax.dot_general(
                queries[own, rows(tile), :], keys, (((1,), (1,)), ((), ())), preferred_element_type=jnp.float32
            )

        def update(tile, scores):
            old = row_max[own, rows(tile), :]
            new = jnp.maximum(old, jnp.broadcast_to(jnp.max(scores, axis=1, keepdims=True), old.shape))
            new = jnp.where(allowed, new, old)
            factor = jnp.exp2((old - new) * SCALE)
            shift = jnp.where(allowed, new * SCALE, 1e30)
            weights = jnp.exp2(scores * scale - shift[:, :1]).astype(jnp.bfloat16)
            total[own, rows(tile), :] = total[own, rows(tile), :] * jnp.concatenate([factor, factor], axis=1) + jnp.dot(
                weights, values, preferred_element_type=jnp.float32
            )
            row_max[own, rows(tile), :] = new

        scores = scores_of(0)
        for tile in range(ROWS // TILE):
            later = scores_of(tile + 1) if tile + 1 < ROWS // TILE else None
            update(tile, scores)
            scores = later

    def finish(own):
        row = lax.broadcasted_iota(jnp.int32, gates.shape, 0) == notes[own, 0, 0:1, 0:1]
        gate = jnp.sum(jnp.where(row, gates[...], 0.0), axis=0, keepdims=True)
        results[own] = (total[own, :, :HD] / total[own, :, HD:] * gate).astype(jnp.bfloat16)
        to_z_lo = core * OWN + own

        def block(which):
            return results.at[own, pl.ds(pl.multiple_of(which * TOK, TOK), TOK), :]

        dst = out.at[:, columns(head)]
        here_or_there(
            z_lo == to_z_lo, block(seq), dst, out_near_send.at[own], out_recv, device(y, z_hi * 4 + to_z_lo, x, core)
        )

        def step(turn, carry):
            which = (seq + turn) % SOURCES
            target = device(y, which // 8 * 4 + to_z_lo, which // 2 % 4, which % 2)
            remote(block(which), dst, out_send.at[own], out_recv, target).start()
            return carry

        lax.fori_loop(1, SOURCES, step, 0)

    note[0] = jnp.full(note.shape[1:], timestep[0], jnp.int32)
    note[1] = jnp.full(note.shape[1:], offsets[0], jnp.int32)
    gate_copy = pltpu.make_async_copy(gate_table.at[:, columns(head)], gates, gate_sem)
    for other in range(2):
        to_z = z_hi * 4 + core * 2 + other
        here_or_there(
            jnp.logical_and(at_home, to_z == z), note, notes.at[mine],
            note_send.at[other], note_recv.at[mine], device(y, to_z, x, home),
        )
    scatter_queries()
    for part in range(PARTS):
        scatter_pairs(part)
    gate_copy.start()
    row_max[...] = jnp.full_like(row_max, -1e30)
    total[...] = jnp.zeros_like(total)
    gate_copy.wait()
    for own in range(OWN):
        wait_bytes(notes.at[own], note_recv.at[own])
        wait_bytes(queries.at[own], query_recv.at[own])

    def stage(index, carry):
        part, block = index // 6, index % 6
        own = 1 - block // 3
        slot = own + WIN - block % 3

        @pl.when(block == 0)
        def _():
            pass_on(1, part)
            pass_on(0, part)

        @pl.when(block == 2)
        def _():
            wait_bytes(pairs.at[1, part], pair_recv.at[1, part])

        @pl.when(block == 4)
        def _():
            wait_bytes(pairs.at[0, part], pair_recv.at[0, part])

        attend(own, slot, part)

        @pl.when(jnp.logical_and(part == PARTS - 1, block % 3 == 2))
        def _():
            finish(own)

        return carry

    lax.fori_loop(0, PARTS * 6, stage, 0)

    wait_bytes(queries.at[:, : ROWS - TOK // 2, :], query_send)
    for part in range(PARTS):
        wait_bytes(pairs.at[:2, part, :, : KEYS - PART // 2, :], pair_send.at[part])
        for own in range(OWN):
            wait_bytes(pairs.at[own, part], chain_send.at[own, part])
    for own in range(OWN):
        wait_bytes(results.at[own, : ROWS - TOK, :], out_send.at[own])

        @pl.when(z_lo != core * OWN + own)
        def _():
            wait_bytes(results.at[own, :TOK, :], out_near_send.at[own])

    for other in range(2):
        @pl.when(jnp.logical_not(jnp.logical_and(at_home, z_hi * 4 + core * 2 + other == z)))
        def _():
            wait_bytes(note, note_send.at[other])

    @pl.when(jnp.logical_not(at_home))
    def _():
        wait_bytes(queries.at[0, :TOK, :], query_near_send)
        for part in range(PARTS):
            wait_bytes(pairs.at[0, part, :, :PART, :], pair_near_send.at[part])

    wait_bytes(out, out_recv)


def body(qkv, timestep, offsets, gate_table):
    stacked = jnp.transpose(qkv[0], (1, 0, 2))
    anywhere = pl.BlockSpec(memory_space=pl.ANY)
    scalar = pl.BlockSpec(memory_space=pltpu.SMEM)
    dma = pltpu.SemaphoreType.DMA
    out = pl.pallas_call(
        kernel,
        out_shape=jax.ShapeDtypeStruct((TOK, qkv.shape[3]), jnp.bfloat16),
        in_specs=[anywhere, scalar, scalar, anywhere],
        out_specs=anywhere,
        scratch_shapes=[
            pltpu.VMEM((OWN, ROWS, HD), jnp.bfloat16),
            pltpu.VMEM((SLOTS, PARTS, 2, KEYS, HD), jnp.bfloat16),
            pltpu.VMEM((OWN, ROWS, HD), jnp.bfloat16),
            pltpu.VMEM((gate_table.shape[0], HD), jnp.float32),
            pltpu.VMEM((2, 8, HD), jnp.int32),
            pltpu.VMEM((OWN, 2, 8, HD), jnp.int32),
            pltpu.VMEM((OWN, ROWS, HD), jnp.float32),
            pltpu.VMEM((OWN, ROWS, 2 * HD), jnp.float32),
            dma((OWN,)),
            dma((SLOTS, PARTS)),
            dma,
            dma((OWN,)),
            dma,
            dma,
            dma((PARTS,)),
            dma((OWN,)),
            dma((2,)),
            dma((OWN, PARTS)),
            dma,
            dma((PARTS,)),
            dma((OWN,)),
        ],
        compiler_params=pltpu.CompilerParams(
            collective_id=0, has_side_effects=True, vmem_limit_bytes=56 * 1024 * 1024
        ),
        cost_estimate=pl.CostEstimate(
            flops=4 * OWN * ROWS * (WIN + 1) * ROWS * HD,
            bytes_accessed=4 * 1024 * 1024,
            transcendentals=OWN * ROWS * (WIN + 1) * ROWS,
        ),
        name="span_attention",
    )(stacked, timestep, offsets, gate_table)
    return out[None]


def solution(mesh):
    return jax.shard_map(
        body,
        mesh=mesh,
        in_specs=(P("span", "seq", None, None), P("span"), P("span"), P()),
        out_specs=P("span", "seq", None),
        check_vma=False,
    )
```

time: 388 us -> 125 us (0.32)
  the two profiles are of different devices: /device:TPU:120 before, /device:TPU:1 now
where the time goes in v2:
time: 125 us; the launch traced here: 123 us
  Pallas kernels  119 us (95%)
  local copies, waits for them, and re-layouts  2.29 us (2%)
  between operations  1.3 us (1%)
    pallas_call x1, Pallas kernels, body(): pl.pallas_call(kernel, out_shape=jax.ShapeDtypeStruct((TOK, qkv.shape[3])...  119 us

profile of v2, /device:TPU:1, one launch (start us, length us, event | category | flops | bytes accessed | tf_op | source)
XLA Modules:
  0.0 122.7 jit_solution(11181592950919004721)
XLA Ops:
  1.3 119.1 %span_attention.1 = bf16[128,4096]{1,0:T(8,128)(2,1)} custom-call(bf16[3,128,4096]{2,1,0:T(8,128)(2,1)} %bitcast.5, s32[1]{0:T(128)S(6)} %copy.6.timestep, s32[1]{0:T(128)S(6)} %copy.7.offsets, f32[50,4096]{1,0:T(8,128)} %gate_table.1), custom_call_target="tpu_custom_call" | custom-call | flops 12884901888 | bytes 4194304 | tf_op jit(solution)/shard_map/span_attention/pallas_call | solution.py:245
  120.5 2.3 %copy.8 = bf16[1,128,4096]{2,1,0:T(8,128)(2,1)} copy(bf16[1,128,4096]{2,1,0:T(8,128)(2,1)} %bitcast.4) | data formatting | bytes 2097152

commit v3 on v2

--- a/solution.py
+++ b/solution.py
@@ -15,10 +15,12 @@
 TOK = 128
 ROWS = SOURCES * TOK
 CHIPS = 32
-PARTS = 2
+PARTS = 4
 PART = TOK // PARTS
 KEYS = SOURCES * PART
 TILE = 256
+SHARES = (80, 48)
+STARTS = (0, SOURCES * 80)
 SCALE = math.log2(math.e) / math.sqrt(HD)
 MESH = pl.DeviceIdType.MESH
 
@@ -88,35 +90,50 @@
         lax.fori_loop(1, CHIPS, step, 0)
 
     mine = z_lo % 2
-    def scatter_queries():
+
+    def query_rows(share, which):
+        size = SHARES[share]
+        return pl.ds(pl.multiple_of(STARTS[share] + which * size, 16), size)
+
+    def token_rows(share):
+        return pl.ds(share * SHARES[0], SHARES[share])
+
+    def scatter_queries(share):
         scatter(
-            lambda which: qkv.at[0, :, columns(which)],
-            queries.at[mine, pl.ds(pl.multiple_of(seq * TOK, TOK), TOK), :],
-            query_send, query_near_send, query_recv.at[mine],
+            lambda which: qkv.at[0, token_rows(share), columns(which)],
+            queries.at[mine, query_rows(share, seq), :],
+            query_send.at[share], query_near_send.at[share], query_recv.at[share, mine],
         )
 
     def scatter_pairs(part):
         scatter(
             lambda which: qkv.at[1:3, pl.ds(part * PART, PART), columns(which)],
-            pairs.at[WIN + mine, part, :, pl.ds(pl.multiple_of(seq * PART, PART), PART), :],
+            pairs.at[part, :, WIN + mine, pl.ds(pl.multiple_of(seq * PART, PART), PART), :],
             pair_send.at[part], pair_near_send.at[part], pair_recv.at[WIN + mine, part],
         )
 
+    def arrived(slot, part):
+        wait_bytes(pairs.at[part, :, slot], pair_recv.at[slot, part])
+
     def pass_on(own, part):
-        wait_bytes(pairs.at[WIN + own, part], pair_recv.at[WIN + own, part])
+        arrived(WIN + own, part)
         remote(
-            pairs.at[WIN + own, part], pairs.at[own, part],
+            pairs.at[part, :, WIN + own], pairs.at[part, :, own],
             chain_send.at[own, part], pair_recv.at[own, part], following,
         ).start()
 
-    def attend(own, slot, part):
-        allowed = first_span + slot - WIN >= notes[own, 1, 0:1, 0:1]
-        scale = jnp.where(allowed, jnp.float32(SCALE), 0.0)
-        keys = pairs[slot, part, 0]
-        values = jnp.concatenate([pairs[slot, part, 1], jnp.ones((KEYS, HD), jnp.bfloat16)], axis=1)
+    def attend(share, own, part):
+        three = pl.ds(own, WIN + 1)
+        first = first_span + own - WIN
+        allowed = [first + step >= notes[own, 1, 0:1, 0:1] for step in range(WIN)]
+        keys = pairs[part, 0, three].reshape((WIN + 1) * KEYS, HD)
+        values = jnp.concatenate(
+            [pairs[part, 1, three].reshape((WIN + 1) * KEYS, HD), jnp.ones(((WIN + 1) * KEYS, HD), jnp.bfloat16)], axis=1
+        )
+        tiles = SOURCES * SHARES[share] // TILE
 
         def rows(tile):
-            return pl.ds(tile * TILE, TILE)
+            return pl.ds(STARTS[share] + tile * TILE, TILE)
 
         def scores_of(tile):
             return lax.dot_general(
@@ -124,41 +141,61 @@
             )
 
         def update(tile, scores):
+            each = [scores[:, step * KEYS : (step + 1) * KEYS] for step in range(WIN + 1)]
+            largest = []
+            for block in each:
+                most = block[:, :HD]
+                for column in range(HD, KEYS, HD):
+                    most = jnp.maximum(most, block[:, column : column + HD])
+                largest.append(most)
+            most = largest[WIN]
+            for step in range(WIN):
+                most = jnp.maximum(most, jnp.where(allowed[step], largest[step], -1e30))
             old = row_max[own, rows(tile), :]
-            new = jnp.maximum(old, jnp.broadcast_to(jnp.max(scores, axis=1, keepdims=True), old.shape))
-            new = jnp.where(allowed, new, old)
+            new = jnp.maximum(old, jnp.broadcast_to(jnp.max(most, axis=1, keepdims=True), old.shape))
             factor = jnp.exp2((old - new) * SCALE)
-            shift = jnp.where(allowed, new * SCALE, 1e30)
-            weights = jnp.exp2(scores * scale - shift[:, :1]).astype(jnp.bfloat16)
+            shift = (new * SCALE)[:, :1]
+            weights = [
+                jnp.exp2(
+                    each[step] * jnp.where(allowed[step], jnp.float32(SCALE), 0.0)
+                    - jnp.where(allowed[step], shift, 1e30)
+                )
+                for step in range(WIN)
+            ]
+            weights.append(jnp.exp2(each[WIN] * SCALE - shift))
             total[own, rows(tile), :] = total[own, rows(tile), :] * jnp.concatenate([factor, factor], axis=1) + jnp.dot(
-                weights, values, preferred_element_type=jnp.float32
+                jnp.concatenate(weights, axis=1).astype(jnp.bfloat16), values, preferred_element_type=jnp.float32
             )
             row_max[own, rows(tile), :] = new
 
         scores = scores_of(0)
-        for tile in range(ROWS // TILE):
-            later = scores_of(tile + 1) if tile + 1 < ROWS // TILE else None
+        for tile in range(tiles):
+            later = scores_of(tile + 1) if tile + 1 < tiles else None
             update(tile, scores)
             scores = later
 
-    def finish(own):
+    def finish(share, own):
+        size = SHARES[share]
+        whole = pl.ds(STARTS[share], SOURCES * size)
         row = lax.broadcasted_iota(jnp.int32, gates.shape, 0) == notes[own, 0, 0:1, 0:1]
         gate = jnp.sum(jnp.where(row, gates[...], 0.0), axis=0, keepdims=True)
-        results[own] = (total[own, :, :HD] / total[own, :, HD:] * gate).astype(jnp.bfloat16)
+        done = total[own, whole, :HD] / total[own, whole, HD:] * gate
+        results[pl.ds(pl.multiple_of(own * ROWS + STARTS[share], TILE), SOURCES * size), :] = done.astype(jnp.bfloat16)
         to_z_lo = core * OWN + own
 
         def block(which):
-            return results.at[own, pl.ds(pl.multiple_of(which * TOK, TOK), TOK), :]
-
-        dst = out.at[:, columns(head)]
+            return results.at[pl.ds(pl.multiple_of(own * ROWS + STARTS[share] + which * size, 16), size), :]
+
+        dst = out.at[token_rows(share), columns(head)]
         here_or_there(
-            z_lo == to_z_lo, block(seq), dst, out_near_send.at[own], out_recv, device(y, z_hi * 4 + to_z_lo, x, core)
+            z_lo == to_z_lo, block(seq), dst, out_near_send.at[share, own], out_recv,
+            device(y, z_hi * 4 + to_z_lo, x, core),
         )
 
         def step(turn, carry):
             which = (seq + turn) % SOURCES
             target = device(y, which // 8 * 4 + to_z_lo, which // 2 % 4, which % 2)
-            remote(block(which), dst, out_send.at[own], out_recv, target).start()
+            remote(block(which), dst, out_send.at[share, own], out_recv, target).start()
             return carry
 
         lax.fori_loop(1, SOURCES, step, 0)
@@ -172,57 +209,75 @@
             jnp.logical_and(at_home, to_z == z), note, notes.at[mine],
             note_send.at[other], note_recv.at[mine], device(y, to_z, x, home),
         )
-    scatter_queries()
+    scatter_queries(0)
     for part in range(PARTS):
         scatter_pairs(part)
+    scatter_queries(1)
     gate_copy.start()
     row_max[...] = jnp.full_like(row_max, -1e30)
     total[...] = jnp.zeros_like(total)
     gate_copy.wait()
+
+    def queries_here(share):
+        for own in range(OWN):
+            wait_bytes(
+                queries.at[own, pl.ds(STARTS[share], SOURCES * SHARES[share]), :], query_recv.at[share, own]
+            )
+
     for own in range(OWN):
         wait_bytes(notes.at[own], note_recv.at[own])
-        wait_bytes(queries.at[own], query_recv.at[own])
-
-    def stage(index, carry):
-        part, block = index // 6, index % 6
-        own = 1 - block // 3
-        slot = own + WIN - block % 3
-
-        @pl.when(block == 0)
-        def _():
-            pass_on(1, part)
-            pass_on(0, part)
-
-        @pl.when(block == 2)
-        def _():
-            wait_bytes(pairs.at[1, part], pair_recv.at[1, part])
-
-        @pl.when(block == 4)
-        def _():
-            wait_bytes(pairs.at[0, part], pair_recv.at[0, part])
-
-        attend(own, slot, part)
-
-        @pl.when(jnp.logical_and(part == PARTS - 1, block % 3 == 2))
-        def _():
-            finish(own)
+    queries_here(0)
+    pass_on(1, 0)
+    pass_on(0, 0)
+
+    def early(index, carry):
+        part, own = index // OWN, 1 - index % OWN
+
+        @pl.when(jnp.logical_and(own == 0, part < PARTS - 1))
+        def _():
+            pass_on(1, part + 1)
+            pass_on(0, part + 1)
+
+        arrived(own, part)
+        attend(0, own, part)
+
+        @pl.when(part == PARTS - 1)
+        def _():
+            finish(0, own)
 
         return carry
 
-    lax.fori_loop(0, PARTS * 6, stage, 0)
-
-    wait_bytes(queries.at[:, : ROWS - TOK // 2, :], query_send)
+    lax.fori_loop(0, PARTS * OWN, early, 0)
+    queries_here(1)
+
+    def late(index, carry):
+        part, own = index % PARTS, 1 - index // PARTS
+        attend(1, own, part)
+
+        @pl.when(part == PARTS - 1)
+        def _():
+            finish(1, own)
+
+        return carry
+
+    lax.fori_loop(0, PARTS * OWN, late, 0)
+
+    def rows_left(count, sem):
+        wait_bytes(results.at[pl.ds(0, count), :], sem)
+
+    for share, size in enumerate(SHARES):
+        for own in range(OWN):
+            rows_left((SOURCES - 1) * size, out_send.at[share, own])
+
+            @pl.when(z_lo != core * OWN + own)
+            def _():
+                rows_left(size, out_near_send.at[share, own])
+
+        rows_left((CHIPS - 1) * size, query_send.at[share])
     for part in range(PARTS):
-        wait_bytes(pairs.at[:2, part, :, : KEYS - PART // 2, :], pair_send.at[part])
+        rows_left((CHIPS - 1) * 2 * PART, pair_send.at[part])
         for own in range(OWN):
-            wait_bytes(pairs.at[own, part], chain_send.at[own, part])
-    for own in range(OWN):
-        wait_bytes(results.at[own, : ROWS - TOK, :], out_send.at[own])
-
-        @pl.when(z_lo != core * OWN + own)
-        def _():
-            wait_bytes(results.at[own, :TOK, :], out_near_send.at[own])
-
+            wait_bytes(pairs.at[part, :, own], chain_send.at[own, part])
     for other in range(2):
         @pl.when(jnp.logical_not(jnp.logical_and(at_home, z_hi * 4 + core * 2 + other == z)))
         def _():
@@ -230,9 +285,10 @@
 
     @pl.when(jnp.logical_not(at_home))
     def _():
-        wait_bytes(queries.at[0, :TOK, :], query_near_send)
+        for share, size in enumerate(SHARES):
+            rows_left(size, query_near_send.at[share])
         for part in range(PARTS):
-            wait_bytes(pairs.at[0, part, :, :PART, :], pair_near_send.at[part])
+            rows_left(2 * PART, pair_near_send.at[part])
 
     wait_bytes(out, out_recv)
 
@@ -249,26 +305,26 @@
         out_specs=anywhere,
         scratch_shapes=[
             pltpu.VMEM((OWN, ROWS, HD), jnp.bfloat16),
-            pltpu.VMEM((SLOTS, PARTS, 2, KEYS, HD), jnp.bfloat16),
-            pltpu.VMEM((OWN, ROWS, HD), jnp.bfloat16),
+            pltpu.VMEM((PARTS, 2, SLOTS, KEYS, HD), jnp.bfloat16),
+            pltpu.VMEM((OWN * ROWS, HD), jnp.bfloat16),
             pltpu.VMEM((gate_table.shape[0], HD), jnp.float32),
             pltpu.VMEM((2, 8, HD), jnp.int32),
             pltpu.VMEM((OWN, 2, 8, HD), jnp.int32),
             pltpu.VMEM((OWN, ROWS, HD), jnp.float32),
             pltpu.VMEM((OWN, ROWS, 2 * HD), jnp.float32),
-            dma((OWN,)),
+            dma((2, OWN)),
             dma((SLOTS, PARTS)),
             dma,
             dma((OWN,)),
             dma,
-            dma,
+            dma((2,)),
             dma((PARTS,)),
-            dma((OWN,)),
+            dma((2, OWN)),
             dma((2,)),
             dma((OWN, PARTS)),
-            dma,
+            dma((2,)),
             dma((PARTS,)),
-            dma((OWN,)),
+            dma((2, OWN)),
         ],
         compiler_params=pltpu.CompilerParams(
             collective_id=0, has_side_effects=True, vmem_limit_bytes=56 * 1024 * 1024

time: 125 us -> 116 us (0.928); the launches traced: 123 us -> 116 us
  Pallas kernels: 119 us -> 112 us
    pallas_call x1, Pallas kernels: 119 us -> 112 us  [body(): pl.pallas_call(kernel, out_shape=jax.ShapeDtypeStruct((TOK, qkv.shape[3])...]
where the time goes in v3:
time: 116 us
  Pallas kernels  112 us (97%)
  local copies, waits for them, and re-layouts  2.29 us (2%)
  between operations  1.3 us (1%)
    pallas_call x1, Pallas kernels, body(): pl.pallas_call(kernel, out_shape=jax.ShapeDtypeStruct((TOK, qkv.shape[3])...  112 us

profile of v3, /device:TPU:1, one launch (start us, length us, event | category | flops | bytes accessed | tf_op | source)
XLA Modules:
  0.0 115.6 jit_solution(13007937800409040376)
XLA Ops:
  1.3 112.0 %span_attention.1 = bf16[128,4096]{1,0:T(8,128)(2,1)} custom-call(bf16[3,128,4096]{2,1,0:T(8,128)(2,1)} %bitcast.5, s32[1]{0:T(128)S(6)} %copy.6.timestep, s32[1]{0:T(128)S(6)} %copy.7.offsets, f32[50,4096]{1,0:T(8,128)} %gate_table.1), custom_call_target="tpu_custom_call" | custom-call | flops 12884901888 | bytes 4194304 | tf_op jit(solution)/shard_map/span_attention/pallas_call | solution.py:301
  113.3 2.3 %copy.8 = bf16[1,128,4096]{2,1,0:T(8,128)(2,1)} copy(bf16[1,128,4096]{2,1,0:T(8,128)(2,1)} %bitcast.4) | data formatting | bytes 2097152

commit v4 on v3

--- a/solution.py
+++ b/solution.py
@@ -19,8 +19,8 @@
 PART = TOK // PARTS
 KEYS = SOURCES * PART
 TILE = 256
-SHARES = (80, 48)
-STARTS = (0, SOURCES * 80)
+SHARES = (96, 32)
+STARTS = (0, SOURCES * 96)
 SCALE = math.log2(math.e) / math.sqrt(HD)
 MESH = pl.DeviceIdType.MESH
 

time: 116 us -> 118 us (1.017)
  Pallas kernels: 112 us -> 114 us
    pallas_call x1, Pallas kernels: 112 us -> 114 us  [body(): pl.pallas_call(kernel, out_shape=jax.ShapeDtypeStruct((TOK, qkv.shape[3])...]
where the time goes in v4:
time: 118 us
  Pallas kernels  114 us (97%)
  local copies, waits for them, and re-layouts  2.29 us (2%)
  between operations  1.3 us (1%)
    pallas_call x1, Pallas kernels, body(): pl.pallas_call(kernel, out_shape=jax.ShapeDtypeStruct((TOK, qkv.shape[3])...  114 us

profile of v4, /device:TPU:1, one launch (start us, length us, event | category | flops | bytes accessed | tf_op | source)
XLA Modules:
  0.0 118.1 jit_solution(17975435826862704570)
XLA Ops:
  1.3 114.5 %span_attention.1 = bf16[128,4096]{1,0:T(8,128)(2,1)} custom-call(bf16[3,128,4096]{2,1,0:T(8,128)(2,1)} %bitcast.5, s32[1]{0:T(128)S(6)} %copy.6.timestep, s32[1]{0:T(128)S(6)} %copy.7.offsets, f32[50,4096]{1,0:T(8,128)} %gate_table.1), custom_call_target="tpu_custom_call" | custom-call | flops 12884901888 | bytes 4194304 | tf_op jit(solution)/shard_map/span_attention/pallas_call | solution.py:301
  115.8 2.3 %copy.8 = bf16[1,128,4096]{2,1,0:T(8,128)(2,1)} copy(bf16[1,128,4096]{2,1,0:T(8,128)(2,1)} %bitcast.4) | data formatting | bytes 2097152
